TPU v7x, 128 devices: a whole 4x4x4 slice. The times are simulated.
128 devices in a mesh: dp: 16 (over x, y_hi, core), pipe: 8 (over z, y_lo).
Axes of the slice: x: 4, y: 4 (y_hi: 2, y_lo: 2; y = y_hi * 2 + y_lo), z: 4, core: 2. Of those that a mesh axis runs over, the one named last changes fastest.
Arguments:
- tokens_in: bfloat16 [8, 2, 2048, 6144], P('pipe', None, 'dp'), may hold values from -6 to 6
- grad_first: bfloat16 [8, 2048, 6144], P('pipe', 'dp'), may hold values from -6 to 6
- grad_last: bfloat16 [2048, 6144], P('dp'), may hold values from -6 to 6
- expert_ids: int32 [8, 2, 2048, 1], P('pipe', None, 'dp'), may hold values from 0 to 1
- gate_probs: float32 [8, 2, 2048], P('pipe', None, 'dp'), may hold values from 0.2 to 1
- w_gate: bfloat16 [8, 2, 6144, 256], P('pipe', None, 'dp'), may hold values from -0.078125 to 0.078125
- w_up: bfloat16 [8, 2, 6144, 256], P('pipe', None, 'dp'), may hold values from -0.078125 to 0.078125
- w_down: bfloat16 [8, 2, 256, 6144], P('pipe', None, None, 'dp'), may hold values from -0.375 to 0.375
Outputs:
- grad_back: bfloat16 [8, 2048, 6144], P('pipe', 'dp')
- d_gate: float32 [8, 2, 6144, 256], P('pipe', None, 'dp')
- d_up: float32 [8, 2, 6144, 256], P('pipe', None, 'dp')
- d_down: float32 [8, 2, 256, 6144], P('pipe', None, None, 'dp')
Inputs may be any that keep to these rules, and one draw needn't show every extreme that they name: `expert_ids`: each token names one expert; every expert is named by some token.
All inputs are finite; a program needn't handle non-finite values.
Results may differ from a plain program's by a relative error of at most 0.017.
Values may be sent and summed in bfloat16 or wider, within the bound.
A program may use at most 192 MiB of HBM per device.

v0:
```python
import math

import jax
import jax.numpy as jnp
from jax import lax
from jax.sharding import PartitionSpec as P


def shifted(x, axis, by):
    length = lax.axis_size(axis)
    pairs = [(i, i + by) for i in range(length) if 0 <= i + by < length]
    return lax.ppermute(x, axis, pairs)


def transpose_dot(left, right):
    return lax.dot_general(
        left, right, (((1,), (1,)), ((), ())), preferred_element_type=jnp.float32
    )


def rows_dot(left, right):
    return lax.dot_general(
        left, right, (((0,), (0,)), ((), ())), preferred_element_type=jnp.float32
    )


def activations(pre_gate, pre_up, down_grad):
    sigmoid_gate = jax.nn.sigmoid(pre_gate)
    silu_gate = pre_gate * sigmoid_gate
    grad_gate = (
        down_grad * pre_up * sigmoid_gate * (1.0 + pre_gate * (1.0 - sigmoid_gate))
    ).astype(jnp.bfloat16)
    grad_up = (down_grad * silu_gate).astype(jnp.bfloat16)
    return (silu_gate * pre_up, grad_gate, grad_up)


def masked_pass(rows_in, rows_grad, expert_of, gates, gate_proj, up_proj, down_proj):
    input_grad = jnp.zeros(rows_in.shape, jnp.float32)
    gate_parts = []
    up_parts = []
    down_parts = []
    for expert in range(gate_proj.shape[0]):
        row_weight = jnp.where(expert_of == expert, gates, jnp.float32(0.0))[:, None]
        pre_gate = jnp.dot(rows_in, gate_proj[expert], preferred_element_type=jnp.float32)
        pre_up = jnp.dot(rows_in, up_proj[expert], preferred_element_type=jnp.float32)
        down_grad = row_weight * transpose_dot(rows_grad, down_proj[expert])
        hidden, grad_gate, grad_up = activations(pre_gate, pre_up, down_grad)
        scaled_hidden = (row_weight * hidden).astype(jnp.bfloat16)
        input_grad = (
            input_grad
            + transpose_dot(grad_gate, gate_proj[expert])
            + transpose_dot(grad_up, up_proj[expert])
        )
        gate_parts.append(rows_dot(rows_in, grad_gate))
        up_parts.append(rows_dot(rows_in, grad_up))
        down_parts.append(rows_dot(scaled_hidden, rows_grad))
    return (input_grad, (jnp.stack(gate_parts), jnp.stack(up_parts), jnp.stack(down_parts)))


def layer_pass(rows_in, rows_grad, expert_of, gates, gate_proj, up_proj, down_proj):
    return masked_pass(rows_in, rows_grad, expert_of, gates, gate_proj, up_proj, down_proj)


def body(tokens_in, grad_first, grad_last, expert_ids, gate_probs, w_gate, w_up, w_down):
    gate_proj, up_proj, down_proj = (
        lax.all_gather(w_gate[0], "dp", axis=1, tiled=True),
        lax.all_gather(w_up[0], "dp", axis=1, tiled=True),
        lax.all_gather(w_down[0], "dp", axis=2, tiled=True),
    )
    tok_rows = tokens_in.shape[2]
    grad_scale = 1.0 / math.sqrt(tok_rows * lax.axis_size("dp"))
    first_grad, first_parts = layer_pass(
        tokens_in[0, 0],
        grad_first[0],
        expert_ids[0, 0, :, 0],
        gate_probs[0, 0],
        gate_proj,
        up_proj,
        down_proj,
    )
    sent = (grad_first[0].astype(jnp.float32) + first_grad).astype(jnp.bfloat16)
    arrived = shifted(sent, "pipe", -1)
    final_section = lax.axis_index("pipe") == lax.axis_size("pipe") - 1
    second_dy = jnp.where(final_section, grad_last, arrived)
    second_grad, second_parts = layer_pass(
        tokens_in[0, 1],
        second_dy,
        expert_ids[0, 1, :, 0],
        gate_probs[0, 1],
        gate_proj,
        up_proj,
        down_proj,
    )
    grad_back = (second_dy.astype(jnp.float32) + second_grad).astype(jnp.bfloat16)
    terms = (
        (first_parts[0] + second_parts[0]) * grad_scale,
        (first_parts[1] + second_parts[1]) * grad_scale,
        (first_parts[2] + second_parts[2]) * grad_scale,
    )
    gate_sum, up_sum, down_sum = (
        lax.psum_scatter(
            terms[0].astype(jnp.bfloat16), "dp", scatter_dimension=1, tiled=True
        ).astype(jnp.float32),
        lax.psum_scatter(
            terms[1].astype(jnp.bfloat16), "dp", scatter_dimension=1, tiled=True
        ).astype(jnp.float32),
        lax.psum_scatter(
            terms[2].astype(jnp.bfloat16), "dp", scatter_dimension=2, tiled=True
        ).astype(jnp.float32),
    )
    return (grad_back[None], gate_sum[None], up_sum[None], down_sum[None])


def solution(mesh):
    placed = (
        P("pipe", None, "dp", None),
        P("pipe", "dp", None),
        P("dp", None),
        P("pipe", None, "dp", None),
        P("pipe", None, "dp"),
        P("pipe", None, "dp", None),
        P("pipe", None, "dp", None),
        P("pipe", None, None, "dp"),
    )
    return jax.shard_map(
        body,
        mesh=mesh,
        in_specs=placed,
        out_specs=(
            P("pipe", "dp", None),
            P("pipe", None, "dp", None),
            P("pipe", None, "dp", None),
            P("pipe", None, None, "dp"),
        ),
        check_vma=False,
    )
```

profile of v0, /device:TPU:105, one launch (start us, length us, event | category | flops | bytes accessed | tf_op | source)
XLA Modules:
  0.0 585.1 jit_solution(2600736361111972416)
XLA Ops:
  7.2 0.7 all-gather.11.cloned.1.call-update
  7.9 0.7 all-gather.9.cloned.1.call-update
  8.7 0.7 all-gather.7.cloned.1.call-update
  9.4 0.8 bitcast_select_fusion
  10.2 65.2 %all-gather.11.cloned.1.call-done = bf16[1,2,6144,256]{3,2,1,0:T(8,128)(2,1)} async-done(((bf16[1,2,384,256]{3,2,1,0:T(8,128)(2,1)}), bf16[1,2,6144,256]{3,2,1,0:T(8,128)(2,1)}) %all-gather.11.cloned.1.call-update) | async-done | bytes 6291472 | tf_op jit(solution)/shard_map/all_gather | solution.py:66
  75.4 2.9 fusion.22
  78.4 62.2 %all-gather.9.cloned.1.call-done = bf16[1,2,6144,256]{3,2,1,0:T(8,128)(2,1)} async-done(((bf16[1,2,384,256]{3,2,1,0:T(8,128)(2,1)}), bf16[1,2,6144,256]{3,2,1,0:T(8,128)(2,1)}) %all-gather.9.cloned.1.call-update) | async-done | bytes 6291472 | tf_op jit(solution)/shard_map/all_gather | solution.py:67
  140.6 3.1 fusion.19
  143.7 67.0 %all-gather.7.cloned.1.call-done = bf16[1,2,256,6144]{3,2,1,0:T(8,128)(2,1)} async-done(((bf16[1,2,256,384]{3,2,1,0:T(8,128)(2,1)}), bf16[1,2,256,6144]{3,2,1,0:T(8,128)(2,1)}) %all-gather.7.cloned.1.call-update) | async-done | bytes 6291472 | tf_op jit(solution)/shard_map/all_gather | solution.py:68
  210.7 3.7 multiply_convert_fusion.8
  214.5 1.0 convolution_bitcast_fusion.10
  215.5 1.0 slice-done.1
  216.5 0.6 fusion.17
  217.1 0.6 fusion.13
  218.3 0.6 slice-done.9
  219.4 1.2 multiply_convert_fusion.10
  220.6 1.2 fusion.16
  221.7 1.2 convolution_add_fusion.5
  222.9 1.2 convolution_add_fusion.4
  224.1 1.2 fusion.7
  225.3 3.3 collective-permute-start
  228.6 1.0 convolution_bitcast_fusion.11
  230.2 0.6 fusion.12
  230.8 0.6 fusion.21
  232.0 29.9 %collective-permute-done = bf16[128,6144]{1,0:T(8,128)(2,1)S(1)} collective-permute-done((bf16[128,6144]{1,0:T(8,128)(2,1)S(1)}, bf16[128,6144]{1,0:T(8,128)(2,1)S(1)}, u32[]{:S(2)}, u32[]{:S(2)}) %collective-permute-start) | collective-permute-done | bytes 1572896 | tf_op jit(solution)/shard_map/ppermute | solution.py:12
  262.1 1.2 multiply_convert_fusion.4
  263.3 1.0 convolution_bitcast_fusion.8
  264.9 0.8 slice-done.11
  265.7 1.2 multiply_convert_fusion.6
  266.9 3.7 convolution_bitcast_fusion.9
  270.6 8.2 %fusion.1 = bf16[2,6144,256]{1,2,0:T(8,128)(2,1)} fusion(f32[1,6144,256]{1,2,0:T(8,128)S(1)} %convolution_bitcast_fusion.10, f32[1,6144,256]{1,2,0:T(8,128)S(1)} %convolution_bitcast_fusion.11, f32[1,6144,256]{1,2,0:T(8,128)S(1)} %convolution_bitcast_fusion.8, f32[1,6144,256]{1,2,0:T(8,128)} %convolution_bitcast_fusion.9), kind=kLoop, calls=%fused_computation.2 | loop fusion | flops 15728640 | bytes 31457280 | tf_op jit(solution)/shard_map/convert_element_type | solution.py:102
  278.7 16.1 %copy.16 = bf16[2,6144,256]{2,0,1:T(2,128)(2,1)} copy(bf16[2,6144,256]{1,2,0:T(8,128)(2,1)} %fusion.1) | data formatting | bytes 12582912
  294.8 6.4 %copy.22 = bf16[768,8,2,256]{3,1,2,0:T(8,128)(2,1)} copy(bf16[768,8,2,256]{3,2,1,0:T(2,128)(2,1)} %bitcast.206) | data formatting | bytes 12582912
  301.6 1.0 convolution_bitcast_fusion.6
  302.5 1.0 convolution_bitcast_fusion.7
  303.5 1.0 convolution_bitcast_fusion.4
  304.6 1.0 convolution_bitcast_fusion.5
  305.6 4.9 fusion.3
  310.5 16.4 %copy.18 = bf16[2,6144,256]{2,0,1:T(2,128)(2,1)} copy(bf16[2,6144,256]{1,2,0:T(8,128)(2,1)} %fusion.3) | data formatting | bytes 12582912
  326.9 6.6 %copy.23 = bf16[768,8,2,256]{3,1,2,0:T(8,128)(2,1)} copy(bf16[768,8,2,256]{3,2,1,0:T(2,128)(2,1)} %bitcast.207) | data formatting | bytes 12582912
  333.9 1.1 copy-done.4
  335.0 1.1 convolution_bitcast_fusion.2
  336.1 1.1 convolution_bitcast_fusion.3
  337.5 1.1 convolution_bitcast_fusion
  338.6 1.1 convolution_bitcast_fusion.1
  339.7 5.0 fusion.5
  344.6 16.1 %copy.20 = bf16[2,256,6144]{1,0,2:T(2,128)(2,1)} copy(bf16[2,256,6144]{2,1,0:T(8,128)(2,1)} %fusion.5) | data formatting | bytes 12582912
  360.8 6.6 %copy.24 = bf16[768,8,2,256]{3,1,2,0:T(8,128)(2,1)} copy(bf16[768,8,2,256]{3,2,1,0:T(2,128)(2,1)} %bitcast.208) | data formatting | bytes 12582912
  367.4 3.2 fusion.14
  370.6 3.2 convolution_add_fusion.2
  373.9 1.2 convolution_add_fusion.1
  375.6 2.4 fusion.20
  377.9 12.7 %reduce-scatter.10.cloned.1.call-done = bf16[384,512]{1,0:T(8,128)(2,1)} async-done(((bf16[6144,512]{1,0:T(8,128)(2,1)}), bf16[384,512]{1,0:T(8,128)(2,1)}) %reduce-scatter.10.cloned.1.call-update) | async-done | bytes 393232
  390.6 1.1 reshape.75
  391.7 0.7 copy.17
  392.5 1.1 copy.14
  393.6 89.5 %reduce-scatter.12.cloned.1.call-done = bf16[384,512]{1,0:T(8,128)(2,1)} async-done(((bf16[6144,512]{1,0:T(8,128)(2,1)}), bf16[384,512]{1,0:T(8,128)(2,1)}) %reduce-scatter.12.cloned.1.call-update) | async-done | bytes 393232
  483.1 1.1 reshape.77
  484.2 0.7 copy.19
  484.9 1.1 copy.15
  486.1 89.5 %reduce-scatter.14.cloned.1.call-done = bf16[384,512]{1,0:T(8,128)(2,1)} async-done(((bf16[6144,512]{1,0:T(8,128)(2,1)}), bf16[384,512]{1,0:T(8,128)(2,1)}) %reduce-scatter.14.cloned.1.call-update) | async-done | bytes 393232
  575.5 1.1 reshape.79
  576.6 0.7 copy.21
  577.3 0.9 bitcast_convert_fusion
  (82 shorter events, 4.7 us)
Async XLA Ops:
  7.2 68.2 %all-gather.11.cloned.1.call-start = ((), (), s32[]{:S(2)}) async-start(), calls=%async_computation.5 | async-start | bytes 6684672 | tf_op jit(solution)/shard_map/all_gather | solution.py:66
  7.9 132.7 %all-gather.9.cloned.1.call-start = ((), (), s32[]{:S(2)}) async-start(), calls=%async_computation.4 | async-start | bytes 6684672 | tf_op jit(solution)/shard_map/all_gather | solution.py:67
  8.6 202.1 %all-gather.7.cloned.1.call-start = ((), (), s32[]{:S(2)}) async-start(), calls=%async_computation.3 | async-start | bytes 6684672 | tf_op jit(solution)/shard_map/all_gather | solution.py:68
  9.4 381.3 %reduce-scatter.10.cloned.1.call-start = ((), (), s32[]{:S(2)}) async-start(), calls=%async_computation.6 | async-start | bytes 6684672
  10.2 130.4 %copy-start = (bf16[1,2,128,6144]{3,2,1,0:T(8,128)(2,1)S(1)}, bf16[1,2,128,6144]{3,2,1,0:T(8,128)(2,1)}, u32[]{:S(2)}) copy-start(bf16[1,2,128,6144]{3,2,1,0:T(8,128)(2,1)} %param.8) | copy-start | bytes 9437188
  78.4 132.4 %copy-start.6 = (f32[128,256]{1,0:T(8,128)}, f32[128,256]{1,0:T(8,128)S(1)}, u32[]{:S(2)}) copy-start(f32[128,256]{1,0:T(8,128)S(1)} %fusion.22) | copy-start | bytes 393220
  210.7 4.7 slice-start
  210.7 6.3 %slice-start.4 = ((s8[6291456]{0:T(1024)(128)(4,1)}), s8[4194304]{0:T(1024)(128)(4,1)S(1)}, s32[]{:S(2)}) async-start(s8[6291456]{0:T(1024)(128)(4,1)} %bitcast.213), calls=%async_computation.13 | async-start | bytes 8388608
  214.4 2.0 slice-start.1
  214.4 2.6 slice-start.5
  214.4 3.8 slice-start.8
  216.5 2.4 slice-start.9
  217.1 0.7 copy-start.9
  217.1 2.3 copy-start.3
  217.7 2.9 copy-start.11
  225.3 36.6 %collective-permute-start = (bf16[128,6144]{1,0:T(8,128)(2,1)S(1)}, bf16[128,6144]{1,0:T(8,128)(2,1)S(1)}, u32[]{:S(2)}, u32[]{:S(2)}) collective-permute-start(bf16[128,6144]{1,0:T(8,128)(2,1)S(1)} %fusion.7), channel_id=1, source_target_pairs={{1,0},{2,1},{3,2},{4,3},{5,4},{6,5},{7,6},{9,8},{10,9},{11,10},{12... | collective-permute-start | bytes 4718600 | tf_op jit(solution)/shard_map/ppermute | solution.py:12
  230.2 34.1 %copy-start.13 = (f32[128,256]{1,0:T(8,128)}, f32[128,256]{1,0:T(8,128)S(1)}, u32[]{:S(2)}) copy-start(f32[128,256]{1,0:T(8,128)S(1)} %fusion.15) | copy-start | bytes 393220
  230.8 33.5 %copy-start.15 = (f32[128,256]{1,0:T(8,128)}, f32[128,256]{1,0:T(8,128)S(1)}, u32[]{:S(2)}) copy-start(f32[128,256]{1,0:T(8,128)S(1)} %fusion.12) | copy-start | bytes 393220
  231.4 30.7 %copy-start.17 = (f32[128,256]{1,0:T(8,128)}, f32[128,256]{1,0:T(8,128)S(1)}, u32[]{:S(2)}) copy-start(f32[128,256]{1,0:T(8,128)S(1)} %fusion.21) | copy-start | bytes 393220
  231.4 30.5 %copy-start.5 = (bf16[128,6144]{1,0:T(8,128)(2,1)S(1)}, bf16[128,6144]{1,0:T(8,128)(2,1)}, u32[]{:S(2)}) copy-start(bf16[128,6144]{1,0:T(8,128)(2,1)} %param.10) | copy-start | bytes 4718596
  232.0 31.3 %copy-start.19 = (f32[128,256]{1,0:T(8,128)}, f32[128,256]{1,0:T(8,128)S(1)}, u32[]{:S(2)}) copy-start(f32[128,256]{1,0:T(8,128)S(1)} %fusion.18) | copy-start | bytes 393220
  262.1 2.3 copy-start.1
  262.1 2.8 slice-start.10
  263.3 2.4 slice-start.11
  301.3 181.8 %reduce-scatter.12.cloned.1.call-start = ((), (), s32[]{:S(2)}) async-start(), calls=%async_computation.7 | async-start | bytes 6684672
  333.6 1.4 copy-start.4
  333.6 1.4 copy-start.7
  333.6 1.4 copy-start.8
  333.6 2.5 copy-start.10
  333.6 242.0 %reduce-scatter.14.cloned.1.call-start = ((), (), s32[]{:S(2)}) async-start(), calls=%async_computation.8 | async-start | bytes 6684672
  335.0 1.1 copy-start.12
  336.1 1.4 copy-start.2
  336.1 1.4 copy-start.18
  336.1 1.4 copy-start.20
  337.5 1.1 copy-start.14
  337.5 1.1 copy-start.16
  367.4 6.5 %slice-start.2 = ((s8[6291456]{0:T(1024)(128)(4,1)}), s8[4194304]{0:T(1024)(128)(4,1)S(1)}, s32[]{:S(2)}) async-start(s8[6291456]{0:T(1024)(128)(4,1)} %bitcast.211), calls=%async_computation.11 | async-start | bytes 8388608
  370.6 3.3 slice-start.3
  370.6 4.4 slice-start.6
  373.9 1.7 slice-start.7
Sparse Core Ops, SparseCore 0:
  10.5 64.8 all-gather.10
  77.9 62.6 all-gather.8
  142.8 67.8 all-gather.6
  301.4 89.1 reduce-scatter.9
  394.6 88.4 reduce-scatter.11
  487.1 88.4 reduce-scatter.13
where the time goes:
time: 590 us; the launch traced here: 585 us
  waiting for transfers between devices  418 us (71%)
  local copies, waits for them, and re-layouts  81.9 us (14%)
  matrix products  46.3 us (8%)
  other arithmetic  20.1 us (3%)
  between operations  14.7 us (2%)
    unnamed x9, waiting for transfers between devices  194 us
    unnamed x80, local copies, waits for them, and re-layouts  81.9 us
    all_gather x1, waiting for transfers between devices, body(): lax.all_gather(w_down[0], 'dp', axis=2, tiled=True)  67 us
    all_gather x1, waiting for transfers between devices, body(): lax.all_gather(w_gate[0], 'dp', axis=1, tiled=True)  65.2 us
    all_gather x1, waiting for transfers between devices, body(): lax.all_gather(w_up[0], 'dp', axis=1, tiled=True)  62.2 us
    ppermute x1, waiting for transfers between devices, shifted(): return lax.ppermute(x, axis, pairs)  29.9 us
    dot_general x12, matrix products, transpose_dot(): lax.dot_general(left, right, (((1,), (1,)), ((), ())), preferred_element_...  21.9 us
    dot_general x12, matrix products, rows_dot(): lax.dot_general(left, right, (((0,), (0,)), ((), ())), preferred_element_...  14.9 us
  transfers between devices with their start and end apart: 7, of which 7 were waited for; matrix products, arithmetic and copies ran while one was open for 15% of the time, Pallas kernels for 0%

commit v1 on v0

v1 whole, which is shorter than its diff:
```python
import functools
import math

import jax
import jax.numpy as jnp
from jax import lax
from jax.experimental import pallas as pl
from jax.experimental.pallas import tpu as pltpu
from jax.sharding import PartitionSpec as P

MESH = pl.DeviceIdType.MESH
BF = jnp.bfloat16
F32 = jnp.float32

NX = 4
CHUNKS = 2


def dot(a, b):
    return lax.dot_general(a, b, (((1,), (0,)), ((), ())), preferred_element_type=F32)


def dot_t(a, b):
    return lax.dot_general(a, b, (((1,), (1,)), ((), ())), preferred_element_type=F32)


class Sems:
    def __init__(self):
        self.count = 0
        self.index = {}

    def __call__(self, *key):
        if key not in self.index:
            self.index[key] = self.count
            self.count += 1
        return self.index[key]


def kernel(
    dims, tok, n_sems,
    x_ref, g1_ref, gl_ref, meta_ref, wg_ref, wu_ref, wd_ref,
    back_ref, dg_ref, du_ref, dd_ref,
    xs, gs, sent, bk, wgu, wdn, metas, msk, prob, xt, sht, act, amask, shm,
    p1gu, r1gu, owngu, s2gu, r2gu, p1d, r1d, ownd, s2d, r2d,
    accgu, accd, pgu, pd, qgu, qd, sem,
):
    wide, half, hid = dims
    n_ch = CHUNKS
    tk = tok // n_ch
    rows = 2 * NX * tk
    four = NX * tk
    tile = min(256, four)
    scale = 1.0 / math.sqrt(tok * lax.axis_size("dp"))

    dp = lax.axis_index("dp")
    sec = lax.axis_index("pipe")
    n_sec = lax.axis_size("pipe")
    x = lax.div(dp, 4)
    yh = lax.rem(lax.div(dp, 2), 2)
    c = lax.rem(dp, 2)
    oc = 1 - c
    block = c * NX + x

    def member(dx, dc):
        px = lax.rem(x + dx, NX)
        pc = lax.rem(c + dc, 2)
        return px, pc, (px * 4 + yh * 2 + pc, sec)

    core_peer = (x * 4 + yh * 2 + oc, sec)
    y_peer = (x * 4 + (1 - yh) * 2 + c, sec)
    before = (dp, lax.rem(sec + n_sec - 1, n_sec))
    after = (dp, lax.rem(sec + 1, n_sec))
    offsets = [(1, 0), (3, 0), (1, 1), (3, 1), (2, 0), (2, 1), (0, 1)]

    names = Sems()
    sends = []

    def s_at(*key):
        return sem.at[names(*key)]

    def rdma(src, dst, ssem, rsem, device):
        pltpu.make_async_remote_copy(
            src_ref=src, dst_ref=dst, send_sem=ssem, recv_sem=rsem,
            device_id=device, device_id_type=MESH,
        ).start()

    def drain(ref, s):
        pltpu.make_async_copy(ref, ref, s).wait()

    def cols_of(px, pc, h):
        return pl.multiple_of(half * (px * 4 + lax.rem(yh + h, 2) * 2 + pc), 128)

    def at(start, size):
        return pl.ds(pl.multiple_of(start, 16), size)

    bar = pltpu.get_barrier_semaphore()
    for dx, dc in offsets:
        pl.semaphore_signal(bar, inc=1, device_id=member(dx, dc)[2], device_id_type=MESH)
    pl.semaphore_signal(bar, inc=1, device_id=y_peer, device_id_type=MESH)
    pl.semaphore_signal(bar, inc=1, device_id=after, device_id_type=MESH)
    pl.semaphore_wait(bar, len(offsets) + 2)

    def spread_meta():
        ss, rs = s_at("meta", "s"), s_at("meta", "r")
        for dx, dc in offsets:
            rdma(meta_ref, metas.at[block], ss, rs, member(dx, dc)[2])
        pltpu.make_async_copy(meta_ref, metas.at[block], rs).start()
        sends.append((ss, metas.at[pl.ds(0, len(offsets))]))

    def masks():
        drain(metas, s_at("meta", "r"))
        for mb in range(2):
            for b in range(2 * NX):
                row = metas[b, mb : mb + 1, :]
                col = jnp.transpose(jnp.broadcast_to(row, (128, 128)))
                for k in range(n_ch):
                    msk[mb, k, b * tk : (b + 1) * tk, :] = col[k * tk : (k + 1) * tk, :]
            row = meta_ref[2 + mb : 3 + mb, :]
            prob[mb] = jnp.transpose(jnp.broadcast_to(row, (128, 128)))

    def weights():
        ss, rs = s_at("wgu", "s"), s_at("wgu", "r")
        for j, (ref, e) in enumerate([(wg_ref, 0), (wg_ref, 1), (wu_ref, 0), (wu_ref, 1)]):
            src = ref.at[0, e]
            cs = pl.ds(j * hid, hid)
            rdma(src, wgu.at[pl.ds(half, half), cs], ss, rs, y_peer)
            pltpu.make_async_copy(src, wgu.at[pl.ds(0, half), cs], rs).start()
        sends.append((ss, wgu.at[pl.ds(0, half)]))
        ss, rs = s_at("wd", "s"), s_at("wd", "r")
        for e in range(2):
            src = wd_ref.at[0, e]
            rr = pl.ds(e * hid, hid)
            rdma(src, wdn.at[rr, pl.ds(half, half)], ss, rs, y_peer)
            pltpu.make_async_copy(src, wdn.at[rr, pl.ds(0, half)], rs).start()
        sends.append((ss, wdn.at[:, pl.ds(0, half)]))

    def spread(src, dst, k, ss, rs):
        for dx, dc in offsets + [(0, 0)]:
            px, pc, device = member(dx, dc)
            for h in range(2):
                a = src.at[pl.ds(k * tk, tk), pl.ds(cols_of(px, pc, h), half)]
                b = dst.at[at(block * tk, tk), pl.ds(h * half, half)]
                if (dx, dc) == (0, 0):
                    pltpu.make_async_copy(a, b, rs).start()
                else:
                    rdma(a, b, ss, rs, device)

    def spread_x(mb, k):
        ss = s_at("x", mb, k, "s")
        spread(x_ref.at[0, mb], xs.at[mb, k], k, ss, s_at("x", mb, k, "r"))
        sends.append((ss, xs.at[mb, k, pl.ds(0, rows - tk)]))

    def spread_g(k):
        ss = s_at("g", 0, k, "s")
        spread(g1_ref.at[0], gs.at[0, k], k, ss, s_at("g", 0, k, "r"))
        sends.append((ss, gs.at[0, k, pl.ds(0, rows - tk)]))

    def spread_last(k):
        @pl.when(sec == n_sec - 1)
        def _():
            spread(gl_ref, gs.at[1, k], k, s_at("last", k, "s"), s_at("g", 1, k, "r"))

    def wait_x(mb, k):
        drain(xs.at[mb, k], s_at("x", mb, k, "r"))

    def wait_g(mb, k):
        drain(gs.at[mb, k], s_at("g", mb, k, "r"))

    def wide_mask(mb, k, start, size):
        m = msk[mb, k, at(start, size), :]
        return jnp.concatenate([m] * (hid // 128), axis=1)

    def pre_gu(mb, k):
        def step(base, out, out_base, kind):
            def one(i, carry):
                r = base + i * tile
                lhs = xs[mb, k, at(r, tile), :]
                second = wide_mask(mb, k, r, tile) != 0.0
                for part in range(2):
                    res = dot(lhs, wgu[:, part * 2 * hid : (part + 1) * 2 * hid])
                    pick = jnp.where(second, res[:, hid:], res[:, :hid])
                    out[mb, k, at(out_base + i * tile, tile), part * hid : (part + 1) * hid] = pick.astype(kind)
                return carry

            lax.fori_loop(0, four // tile, one, 0)

        step(oc * four, p1gu, 0, BF)
        ss = s_at("p1gu", mb, k, "s")
        rdma(p1gu.at[mb, k], r1gu.at[mb, k], ss, s_at("p1gu", mb, k, "r"), core_peer)
        sends.append((ss, p1gu.at[mb, k]))
        step(c * four, owngu, 0, F32)

    def pre_d(mb, k):
        def step(base, out, kind):
            def one(i, carry):
                r = base + i * tile
                res = dot_t(gs[mb, k, at(r, tile), :], wdn[...])
                second = wide_mask(mb, k, r, tile) != 0.0
                pick = jnp.where(second, res[:, hid:], res[:, :hid])
                out[mb, k, at(i * tile, tile), :] = pick.astype(kind)
                return carry

            lax.fori_loop(0, four // tile, one, 0)

        step(oc * four, p1d, BF)
        ss = s_at("p1d", mb, k, "s")
        rdma(p1d.at[mb, k], r1d.at[mb, k], ss, s_at("p1d", mb, k, "r"), core_peer)
        sends.append((ss, p1d.at[mb, k]))
        step(c * four, ownd, F32)

    def along_x(tag, own, r1, s2, r2, mb, k):
        drain(r1.at[mb, k], s_at("p1" + tag, mb, k, "r"))
        ss, rs = s_at("s2" + tag, mb, k, "s"), s_at("s2" + tag, mb, k, "r")
        for dx in (2, 1, 3):
            px, _, device = member(dx, 0)
            rr = at(px * tk, tk)
            s2[mb, k, dx - 1] = (own[mb, k, rr, :] + r1[mb, k, rr, :].astype(F32)).astype(BF)
            rdma(s2.at[mb, k, dx - 1], r2.at[mb, k, dx - 1], ss, rs, device)
        sends.append((ss, s2.at[mb, k]))

    def mid_gu(mb, k):
        along_x("gu", owngu, r1gu, s2gu, r2gu, mb, k)

    def mid_d(mb, k):
        along_x("d", ownd, r1d, s2d, r2d, mb, k)

    def total(tag, own, r1, r2, mb, k):
        drain(r2.at[mb, k], s_at("s2" + tag, mb, k, "r"))
        rr = at(x * tk, tk)
        res = own[mb, k, rr, :] + r1[mb, k, rr, :].astype(F32)
        for dx in range(NX - 1):
            res = res + r2[mb, k, dx].astype(F32)
        return res

    def activate(mb, k):
        gu = total("gu", owngu, r1gu, r2gu, mb, k)
        dn = total("d", ownd, r1d, r2d, mb, k)
        p = prob[mb, k * tk : (k + 1) * tk, :]
        p = jnp.concatenate([p] * (hid // 128), axis=1)
        gate, up = gu[:, :hid], gu[:, hid:]
        down = p * dn
        sig = jax.nn.sigmoid(gate)
        silu = gate * sig
        mine = at(block * tk, tk)
        act[mb, k, mine, 0:hid] = (down * up * sig * (1.0 + gate * (1.0 - sig))).astype(BF)
        act[mb, k, mine, hid : 2 * hid] = (down * silu).astype(BF)
        act[mb, k, mine, 2 * hid : 3 * hid] = (p * (silu * up)).astype(BF)
        ss, rs = s_at("ag", mb, k, "s"), s_at("ag", mb, k, "r")
        piece = act.at[mb, k, mine]
        for dx in (2, 1, 3):
            rdma(piece, piece, ss, rs, member(dx, 0)[2])
        sends.append((ss, act.at[mb, k, pl.ds(0, 3 * tk)]))

    def forward(mb, k):
        drain(act.at[mb, k, pl.ds(0, 3 * tk)], s_at("ag", mb, k, "r"))
        ss = s_at("fw", mb, k, "s")
        piece = act.at[mb, k, at(c * four, four)]
        rdma(piece, piece, ss, s_at("fw", mb, k, "r"), core_peer)
        sends.append((ss, act.at[mb, k, pl.ds(0, four)]))

    def spread_acts(mb, k):
        drain(act.at[mb, k, pl.ds(0, four)], s_at("fw", mb, k, "r"))

        def one(i, carry):
            r = at(i * tile, tile)
            second = wide_mask(mb, k, i * tile, tile)
            first = 1.0 - second
            for j in range(3):
                a = act[mb, k, r, j * hid : (j + 1) * hid].astype(F32)
                lo, hi = (a * first).astype(BF), (a * second).astype(BF)
                if j < 2:
                    amask[mb, k, r, 2 * j * hid : (2 * j + 1) * hid] = lo
                    amask[mb, k, r, (2 * j + 1) * hid : (2 * j + 2) * hid] = hi
                else:
                    shm[mb, k, r, 0:hid] = lo
                    shm[mb, k, r, hid : 2 * hid] = hi
            return carry

        lax.fori_loop(0, rows // tile, one, 0)

    def new_grad(mb, k, r, size):
        rr = at(r, size)
        res = dot_t(amask[mb, k, rr, :], wgu[...])
        return (gs[mb, k, rr, :].astype(F32) + res).astype(BF)

    def relay(k):
        @pl.when(sec > 0)
        def _():
            def one(i, carry):
                r = at(i * tile, tile)
                sent[k, r, :] = new_grad(0, k, i * tile, tile)
                rdma(sent.at[k, r], gs.at[1, k, r], s_at("shift", k, "s"), s_at("g", 1, k, "r"), before)
                return carry

            lax.fori_loop(0, rows // tile, one, 0)

    def give_back(k):
        ss, rs = s_at("back", k, "s"), s_at("back", k, "r")
        for dx, dc in [(2, 0), (2, 1), (1, 0), (1, 1), (3, 0), (3, 1), (0, 1), (0, 0)]:
            px, pc, device = member(dx, dc)
            pos = (pc * NX + px) * tk
            bk[k, at(pos, tk), :] = new_grad(1, k, pos, tk)
            for h in range(2):
                a = bk.at[k, at(pos, tk), pl.ds(h * half, half)]
                b = back_ref.at[0, pl.ds(k * tk, tk), pl.ds(cols_of(x, c, h), half)]
                if (dx, dc) == (0, 0):
                    pltpu.make_async_copy(a, b, rs).start()
                else:
                    rdma(a, b, ss, rs, device)
        sends.append((ss, bk.at[k, pl.ds(0, rows - tk)]))

    def turn_x(mb, k):
        for i in range(wide // 256):
            xt[i * 256 : (i + 1) * 256, :] = jnp.transpose(xs[mb, k, :, i * 256 : (i + 1) * 256])

    def turn_s(mb, k):
        for i in range(2 * hid // 256):
            sht[i * 256 : (i + 1) * 256, :] = jnp.transpose(shm[mb, k, :, i * 256 : (i + 1) * 256])

    def grads(mb, k, first, last):
        turn_x(mb, k)
        turn_s(mb, k)
        for h in (1, 0):
            hs = slice(h * half, (h + 1) * half)
            for j in range(4):
                cs = slice(j * hid, (j + 1) * hid)
                res = dot(xt[hs, :], amask[mb, k, :, cs])
                if not first:
                    res = res + accgu[hs, cs]
                if last and h == 1:
                    pgu[j] = (res * scale).astype(BF)
                    ss = s_at("pgu", j, "s")
                    rdma(pgu.at[j], qgu.at[j], ss, s_at("pgu", j, "r"), y_peer)
                    sends.append((ss, pgu.at[j]))
                else:
                    accgu[hs, cs] = res
            for e in range(2):
                es = slice(e * hid, (e + 1) * hid)
                res = dot(sht[es, :], gs[mb, k, :, hs])
                if not first:
                    res = res + accd[es, hs]
                if last and h == 1:
                    pd[e] = (res * scale).astype(BF)
                    ss = s_at("pd", e, "s")
                    rdma(pd.at[e], qd.at[e], ss, s_at("pd", e, "r"), y_peer)
                    sends.append((ss, pd.at[e]))
                else:
                    accd[es, hs] = res

    def finish():
        for j, (ref, e) in enumerate([(dg_ref, 0), (dg_ref, 1), (du_ref, 0), (du_ref, 1)]):
            drain(qgu.at[j], s_at("pgu", j, "r"))
            ref[0, e] = accgu[0:half, j * hid : (j + 1) * hid] * scale + qgu[j].astype(F32)
        for e in range(2):
            drain(qd.at[e], s_at("pd", e, "r"))
            dd_ref[0, e] = accd[e * hid : (e + 1) * hid, 0:half] * scale + qd[e].astype(F32)

    spread_meta()
    weights()
    for k in range(n_ch):
        spread_x(0, k)
        spread_g(k)
    masks()
    drain(wgu, s_at("wgu", "r"))
    drain(wdn, s_at("wd", "r"))
    for k in range(n_ch):
        wait_x(0, k)
        pre_gu(0, k)
        wait_g(0, k)
        pre_d(0, k)
        mid_gu(0, k)
        mid_d(0, k)
        if k > 0:
            activate(0, k - 1)
    activate(0, n_ch - 1)
    for k in range(n_ch):
        spread_x(1, k)
        spread_last(k)
    for k in range(n_ch):
        forward(0, k)
        spread_acts(0, k)
        relay(k)
    for k in range(n_ch):
        grads(0, k, k == 0, False)
    for k in range(n_ch):
        wait_x(1, k)
        pre_gu(1, k)
        mid_gu(1, k)
    for k in range(n_ch):
        wait_g(1, k)
        pre_d(1, k)
        mid_d(1, k)
        activate(1, k)
        forward(1, k)
        spread_acts(1, k)
        if k < n_ch - 1:
            give_back(k)
        grads(1, k, False, k == n_ch - 1)
        if k == n_ch - 1:
            give_back(k)
    finish()
    for k in range(n_ch):
        @pl.when(sec > 0)
        def _():
            drain(sent.at[k], s_at("shift", k, "s"))

        @pl.when(sec == n_sec - 1)
        def _():
            drain(gs.at[1, k, pl.ds(0, rows - tk)], s_at("last", k, "s"))
        drain(bk.at[k], s_at("back", k, "r"))
    for s, ref in sends:
        drain(ref, s)
    assert names.count <= n_sems, names.count


def body(tokens_in, grad_first, grad_last, expert_ids, gate_probs, w_gate, w_up, w_down):
    tok, width = tokens_in.shape[2:]
    half, hid = w_gate.shape[2:]
    wide = 2 * half
    tk = tok // CHUNKS
    rows, four = 2 * NX * tk, NX * tk
    meta = jnp.concatenate(
        [expert_ids[0, :, :, 0].astype(F32), gate_probs[0], jnp.zeros((4, tok), F32)], axis=0
    )
    n_sems = 40 + 44 * CHUNKS
    pair = (2, CHUNKS)
    scratch = [
        pltpu.VMEM(pair + (rows, wide), BF),
        pltpu.VMEM(pair + (rows, wide), BF),
        pltpu.VMEM((CHUNKS, rows, wide), BF),
        pltpu.VMEM((CHUNKS, rows, wide), BF),
        pltpu.VMEM((wide, 4 * hid), BF),
        pltpu.VMEM((2 * hid, wide), BF),
        pltpu.VMEM((2 * NX, 8, tok), F32),
        pltpu.VMEM(pair + (rows, 128), F32),
        pltpu.VMEM((2, tok, 128), F32),
        pltpu.VMEM((wide, rows), BF),
        pltpu.VMEM((2 * hid, rows), BF),
        pltpu.VMEM(pair + (rows, 3 * hid), BF),
        pltpu.VMEM(pair + (rows, 4 * hid), BF),
        pltpu.VMEM(pair + (rows, 2 * hid), BF),
    ]
    for cols in (2 * hid, hid):
        scratch += [
            pltpu.VMEM(pair + (four, cols), BF),
            pltpu.VMEM(pair + (four, cols), BF),
            pltpu.VMEM(pair + (four, cols), F32),
            pltpu.VMEM(pair + (NX - 1, tk, cols), BF),
            pltpu.VMEM(pair + (NX - 1, tk, cols), BF),
        ]
    scratch += [
        pltpu.VMEM((wide, 4 * hid), F32),
        pltpu.VMEM((2 * hid, wide), F32),
        pltpu.VMEM((4, half, hid), BF),
        pltpu.VMEM((2, hid, half), BF),
        pltpu.VMEM((4, half, hid), BF),
        pltpu.VMEM((2, hid, half), BF),
        pltpu.SemaphoreType.DMA((n_sems,)),
    ]
    vmem = pl.BlockSpec(memory_space=pltpu.VMEM)
    hbm = pl.BlockSpec(memory_space=pl.ANY)
    return pl.pallas_call(
        functools.partial(kernel, (wide, half, hid), tok, n_sems),
        out_shape=(
            jax.ShapeDtypeStruct((1, tok, width), BF),
            jax.ShapeDtypeStruct(w_gate.shape, F32),
            jax.ShapeDtypeStruct(w_up.shape, F32),
            jax.ShapeDtypeStruct(w_down.shape, F32),
        ),
        in_specs=[hbm, hbm, hbm, vmem, hbm, hbm, hbm],
        out_specs=(vmem,) * 4,
        scratch_shapes=scratch,
        compiler_params=pltpu.CompilerParams(
            collective_id=0, has_side_effects=True, vmem_limit_bytes=60 << 20
        ),
        name="section",
    )(tokens_in, grad_first, grad_last, meta, w_gate, w_up, w_down)


def solution(mesh):
    placed = (
        P("pipe", None, "dp", None),
        P("pipe", "dp", None),
        P("dp", None),
        P("pipe", None, "dp", None),
        P("pipe", None, "dp"),
        P("pipe", None, "dp", None),
        P("pipe", None, "dp", None),
        P("pipe", None, None, "dp"),
    )
    return jax.shard_map(
        body,
        mesh=mesh,
        in_specs=placed,
        out_specs=(
            P("pipe", "dp", None),
            P("pipe", None, "dp", None),
            P("pipe", None, "dp", None),
            P("pipe", None, None, "dp"),
        ),
        check_vma=False,
    )
```

time: 590 us -> 168 us (0.28)
  waiting for transfers between devices: 418 us -> 0 us
  Pallas kernels: 0 us -> 159 us
  local copies, waits for them, and re-layouts: 81.9 us -> 6.02 us
  matrix products: 46.3 us -> 0 us
  other arithmetic: 20.1 us -> 2.02 us
  between operations: 14.7 us -> 0.66 us
    all_gather x3 -> x0, waiting for transfers between devices: 194 us -> none  [the longest x1 67 us: body(): lax.all_gather(w_down[0], 'dp', axis=2, tiled=True)]
    unnamed x9 -> x0, waiting for transfers between devices: 194 us -> none
    pallas_call x0 -> x1, Pallas kernels: none -> 159 us  [body(): pl.pallas_call(functools.partial(kernel, (wide, half, hid), tok, n_sems),...]
    unnamed x80 -> x10, local copies, waits for them, and re-layouts: 81.9 us -> 5.94 us
    dot_general x32 -> x0, matrix products: 46.3 us -> none  [the longest x12 21.9 us: transpose_dot(): lax.dot_general(left, right, (((1,), (1,)), ((), ())), preferred_element_...]
    ppermute x1 -> x0, waiting for transfers between devices: 29.9 us -> none  [shifted(): return lax.ppermute(x, axis, pairs)]
    convert_element_type x3 -> x1, other arithmetic: 18.1 us -> 0.68 us  [body(): expert_ids[0, :, :, 0].astype(F32)]
  transfers between devices with their start and end apart: 7 -> 0, of which waited for: 7 -> 0; matrix products, arithmetic and copies ran while one was open for 15% -> 0% of each run, Pallas kernels for 0% -> 0%
where the time goes in v1:
time: 168 us
  Pallas kernels  159 us (95%)
  local copies, waits for them, and re-layouts  6.02 us (4%)
  other arithmetic  2.02 us (1%)
    pallas_call x1, Pallas kernels, body(): pl.pallas_call(functools.partial(kernel, (wide, half, hid), tok, n_sems),...  159 us
    unnamed x10, local copies, waits for them, and re-layouts  5.94 us

profile of v1, /device:TPU:105, one launch (start us, length us, event | category | flops | bytes accessed | tf_op | source)
XLA Modules:
  0.0 167.8 jit_solution(11153926149583634784)
XLA Ops:
  0.6 0.1 pad.2.clone
  0.7 0.7 convert_bitcast_fusion
  1.4 1.3 maximum_maximum_fusion.meta_ref
  2.7 159.1 %section.1 = (bf16[1,128,6144]{2,1,0:T(8,128)(2,1)}, f32[1,2,384,256]{3,2,1,0:T(8,128)}, f32[1,2,384,256]{3,2,1,0:T(8,128)}, f32[1,2,256,384]{3,2,1,0:T(8,128)}) custom-call(bf16[1,2,128,6144]{3,2,1,0:T(8,128)(2,1)} %x_ref.1, bf16[1,128,6144]{2,1,0:T(8,128)(2,1)} %g1_ref.1, bf16[128,6144]{1,0:T(8,128)(2,1)} %gl_ref.1, ...), custom_call_target="tpu_custom_call" | custom-call | tf_op jit(solution)/shard_map/section/pallas_call | solution.py:462
  161.9 0.0 copy-start.2
  161.9 2.8 %copy.17 = bf16[1,128,6144]{2,1,0:T(8,128)(2,1)} copy(bf16[1,128,6144]{2,1,0:T(8,128)(2,1)} %get-tuple-element.8) | data formatting | bytes 3145728
  164.7 0.0 copy-done.2
  164.7 0.0 copy-start.1
  164.7 0.0 copy-start
  164.7 0.9 copy.18
  165.6 0.5 copy-done.1
  166.1 0.9 copy.19
  167.0 0.0 copy-done
  167.0 0.9 copy.20
  (1 shorter events, 0.0 us)
Async XLA Ops:
  161.9 2.8 %copy-start.2 = (f32[1,2,384,256]{3,2,1,0:T(8,128)S(1)}, f32[1,2,384,256]{3,2,1,0:T(8,128)}, u32[]{:S(2)}) copy-start(f32[1,2,384,256]{3,2,1,0:T(8,128)} %get-tuple-element.9) | copy-start | bytes 2359300
  164.7 1.4 copy-start.1
  164.7 2.3 %copy-start = (f32[1,2,256,384]{3,2,1,0:T(8,128)S(1)}, f32[1,2,256,384]{3,2,1,0:T(8,128)}, u32[]{:S(2)}) copy-start(f32[1,2,256,384]{3,2,1,0:T(8,128)} %get-tuple-element.11) | copy-start | bytes 2359300

commit v2 on v1

--- a/solution.py
+++ b/solution.py
@@ -36,11 +36,30 @@
         return self.index[key]
 
 
+ORDER = [
+    ("spread_meta",), ("weights_gu",), ("spread_x", 0, 0), ("spread_g", 0), ("weights_d",), ("masks",),
+    ("wait_x", 0, 0), ("spread_x", 0, 1), ("spread_last",),
+    ("wait_gu",), ("pre_gu", 0, 0), ("mid_gu", 0, 0), ("turn_x", 0, 0), ("wait_g", 0, 0), ("wait_d",), ("pre_d", 0, 0), ("mid_d", 0, 0),
+    ("wait_x", 0, 1), ("pre_gu", 0, 1), ("activate", 0, 0), ("spread_g", 1), ("mid_gu", 0, 1), ("relay_last",),
+    ("forward", 0, 0), ("spread_acts", 0, 0), ("relay", 0),
+    ("turn_x", 0, 1), ("wait_g", 0, 1), ("pre_d", 0, 1), ("mid_d", 0, 1), ("activate", 0, 1), ("spread_x", 1, 0),
+    ("forward", 0, 1), ("spread_x", 1, 1), ("spread_acts", 0, 1), ("relay", 1), ("grads", 0, 0), ("grads", 0, 1),
+    ("wait_x", 1, 0), ("pre_gu", 1, 0), ("mid_gu", 1, 0), ("turn_x", 1, 0), ("wait_g", 1, 0), ("pre_d", 1, 0), ("mid_d", 1, 0),
+    ("wait_x", 1, 1), ("pre_gu", 1, 1), ("mid_gu", 1, 1), ("activate", 1, 0), ("turn_x", 1, 1),
+    ("wait_g", 1, 1), ("pre_d", 1, 1), ("forward", 1, 0), ("mid_d", 1, 1), ("spread_acts", 1, 0),
+    ("activate", 1, 1), ("grads", 1, 0), ("forward", 1, 1), ("spread_acts", 1, 1), ("grads", 1, 1), ("give_back", 0), ("give_back", 1), ("finish",),
+]
+
+
+def schedule(n):
+    return ORDER
+
+
 def kernel(
     dims, tok, n_sems,
-    x_ref, g1_ref, gl_ref, meta_ref, wg_ref, wu_ref, wd_ref,
+    x_ref, g1_ref, gl_ref, ids_ref, p_ref, wg_ref, wu_ref, wd_ref,
     back_ref, dg_ref, du_ref, dd_ref,
-    xs, gs, sent, bk, wgu, wdn, metas, msk, prob, xt, sht, act, amask, shm,
+    xs, gs, glq, sent, bk, wgu, wdn, metas, msk, prob, xt, sht, act, amask, shm,
     p1gu, r1gu, owngu, s2gu, r2gu, p1d, r1d, ownd, s2d, r2d,
     accgu, accd, pgu, pd, qgu, qd, sem,
 ):
@@ -98,27 +117,34 @@
         pl.semaphore_signal(bar, inc=1, device_id=member(dx, dc)[2], device_id_type=MESH)
     pl.semaphore_signal(bar, inc=1, device_id=y_peer, device_id_type=MESH)
     pl.semaphore_signal(bar, inc=1, device_id=after, device_id_type=MESH)
-    pl.semaphore_wait(bar, len(offsets) + 2)
+
+    @pl.when(sec == n_sec - 1)
+    def _():
+        for q in range(3):
+            pl.semaphore_signal(bar, inc=1, device_id=(dp, 2 * q + 1), device_id_type=MESH)
+
+    helper = jnp.where((lax.rem(sec, 2) == 1) & (sec < n_sec - 1), 1, 0)
+    pl.semaphore_wait(bar, len(offsets) + 2 + helper)
 
     def spread_meta():
         ss, rs = s_at("meta", "s"), s_at("meta", "r")
         for dx, dc in offsets:
-            rdma(meta_ref, metas.at[block], ss, rs, member(dx, dc)[2])
-        pltpu.make_async_copy(meta_ref, metas.at[block], rs).start()
+            rdma(ids_ref, metas.at[block], ss, rs, member(dx, dc)[2])
+        pltpu.make_async_copy(ids_ref, metas.at[block], rs).start()
         sends.append((ss, metas.at[pl.ds(0, len(offsets))]))
 
     def masks():
         drain(metas, s_at("meta", "r"))
         for mb in range(2):
             for b in range(2 * NX):
-                row = metas[b, mb : mb + 1, :]
+                row = metas[b, mb : mb + 1, :].astype(F32)
                 col = jnp.transpose(jnp.broadcast_to(row, (128, 128)))
                 for k in range(n_ch):
                     msk[mb, k, b * tk : (b + 1) * tk, :] = col[k * tk : (k + 1) * tk, :]
-            row = meta_ref[2 + mb : 3 + mb, :]
+            row = p_ref[mb : mb + 1, :]
             prob[mb] = jnp.transpose(jnp.broadcast_to(row, (128, 128)))
 
-    def weights():
+    def weights_gu():
         ss, rs = s_at("wgu", "s"), s_at("wgu", "r")
         for j, (ref, e) in enumerate([(wg_ref, 0), (wg_ref, 1), (wu_ref, 0), (wu_ref, 1)]):
             src = ref.at[0, e]
@@ -126,6 +152,8 @@
             rdma(src, wgu.at[pl.ds(half, half), cs], ss, rs, y_peer)
             pltpu.make_async_copy(src, wgu.at[pl.ds(0, half), cs], rs).start()
         sends.append((ss, wgu.at[pl.ds(0, half)]))
+
+    def weights_d():
         ss, rs = s_at("wd", "s"), s_at("wd", "r")
         for e in range(2):
             src = wd_ref.at[0, e]
@@ -134,31 +162,59 @@
             pltpu.make_async_copy(src, wdn.at[rr, pl.ds(0, half)], rs).start()
         sends.append((ss, wdn.at[:, pl.ds(0, half)]))
 
-    def spread(src, dst, k, ss, rs):
+    def wait_gu():
+        drain(wgu, s_at("wgu", "r"))
+
+    def wait_d():
+        drain(wdn, s_at("wd", "r"))
+
+    def spread(src, dst, start, size, place, ss, rs):
         for dx, dc in offsets + [(0, 0)]:
             px, pc, device = member(dx, dc)
             for h in range(2):
-                a = src.at[pl.ds(k * tk, tk), pl.ds(cols_of(px, pc, h), half)]
-                b = dst.at[at(block * tk, tk), pl.ds(h * half, half)]
+                a = src.at[pl.ds(start, size), pl.ds(cols_of(px, pc, h), half)]
+                b = dst.at[at(place, size), pl.ds(h * half, half)]
                 if (dx, dc) == (0, 0):
                     pltpu.make_async_copy(a, b, rs).start()
                 else:
                     rdma(a, b, ss, rs, device)
 
     def spread_x(mb, k):
-        ss = s_at("x", mb, k, "s")
-        spread(x_ref.at[0, mb], xs.at[mb, k], k, ss, s_at("x", mb, k, "r"))
-        sends.append((ss, xs.at[mb, k, pl.ds(0, rows - tk)]))
+        ss = s_at("x", "s")
+        spread(x_ref.at[0, mb], xs.at[mb, k], k * tk, tk, block * tk, ss, s_at("x", mb, k, "r"))
 
     def spread_g(k):
-        ss = s_at("g", 0, k, "s")
-        spread(g1_ref.at[0], gs.at[0, k], k, ss, s_at("g", 0, k, "r"))
-        sends.append((ss, gs.at[0, k, pl.ds(0, rows - tk)]))
-
-    def spread_last(k):
-        @pl.when(sec == n_sec - 1)
-        def _():
-            spread(gl_ref, gs.at[1, k], k, s_at("last", k, "s"), s_at("g", 1, k, "r"))
+        ss = s_at("g", "s")
+        spread(g1_ref.at[0], gs.at[0, k], k * tk, tk, block * tk, ss, s_at("g", 0, k, "r"))
+
+    def quarter(q):
+        per = 4 // n_ch
+        size = tk // per
+        return q // per, (q % per) * size, size
+
+    def spread_last():
+        for q in range(4):
+            @pl.when(sec == 2 * q + 1)
+            def _():
+                k, base, size = quarter(q)
+                if q < 3:
+                    rs = s_at("lastq", "r")
+                    spread(gl_ref, glq, k * tk + base, size, block * size, s_at("last", "s"), rs)
+                else:
+                    rs = s_at("g", 1, k, "r")
+                    spread(gl_ref, gs.at[1, k], k * tk + base, size, block * tk + base, s_at("last", "s"), rs)
+
+    def relay_last():
+        for q in range(3):
+            @pl.when(sec == 2 * q + 1)
+            def _():
+                k, base, size = quarter(q)
+                drain(glq, s_at("lastq", "r"))
+                for b in range(2 * NX):
+                    rdma(
+                        glq.at[pl.ds(b * size, size)], gs.at[1, k, pl.ds(b * tk + base, size)],
+                        s_at("lastq", "s"), s_at("g", 1, k, "r"), (dp, n_sec - 1),
+                    )
 
     def wait_x(mb, k):
         drain(xs.at[mb, k], s_at("x", mb, k, "r"))
@@ -185,9 +241,8 @@
             lax.fori_loop(0, four // tile, one, 0)
 
         step(oc * four, p1gu, 0, BF)
-        ss = s_at("p1gu", mb, k, "s")
+        ss = s_at("p1gu", "s")
         rdma(p1gu.at[mb, k], r1gu.at[mb, k], ss, s_at("p1gu", mb, k, "r"), core_peer)
-        sends.append((ss, p1gu.at[mb, k]))
         step(c * four, owngu, 0, F32)
 
     def pre_d(mb, k):
@@ -203,20 +258,18 @@
             lax.fori_loop(0, four // tile, one, 0)
 
         step(oc * four, p1d, BF)
-        ss = s_at("p1d", mb, k, "s")
+        ss = s_at("p1d", "s")
         rdma(p1d.at[mb, k], r1d.at[mb, k], ss, s_at("p1d", mb, k, "r"), core_peer)
-        sends.append((ss, p1d.at[mb, k]))
         step(c * four, ownd, F32)
 
     def along_x(tag, own, r1, s2, r2, mb, k):
         drain(r1.at[mb, k], s_at("p1" + tag, mb, k, "r"))
-        ss, rs = s_at("s2" + tag, mb, k, "s"), s_at("s2" + tag, mb, k, "r")
+        ss, rs = s_at("s2" + tag, "s"), s_at("s2" + tag, mb, k, "r")
         for dx in (2, 1, 3):
             px, _, device = member(dx, 0)
             rr = at(px * tk, tk)
             s2[mb, k, dx - 1] = (own[mb, k, rr, :] + r1[mb, k, rr, :].astype(F32)).astype(BF)
             rdma(s2.at[mb, k, dx - 1], r2.at[mb, k, dx - 1], ss, rs, device)
-        sends.append((ss, s2.at[mb, k]))
 
     def mid_gu(mb, k):
         along_x("gu", owngu, r1gu, s2gu, r2gu, mb, k)
@@ -245,18 +298,16 @@
         act[mb, k, mine, 0:hid] = (down * up * sig * (1.0 + gate * (1.0 - sig))).astype(BF)
         act[mb, k, mine, hid : 2 * hid] = (down * silu).astype(BF)
         act[mb, k, mine, 2 * hid : 3 * hid] = (p * (silu * up)).astype(BF)
-        ss, rs = s_at("ag", mb, k, "s"), s_at("ag", mb, k, "r")
+        ss, rs = s_at("ag", "s"), s_at("ag", mb, k, "r")
         piece = act.at[mb, k, mine]
         for dx in (2, 1, 3):
             rdma(piece, piece, ss, rs, member(dx, 0)[2])
-        sends.append((ss, act.at[mb, k, pl.ds(0, 3 * tk)]))
 
     def forward(mb, k):
         drain(act.at[mb, k, pl.ds(0, 3 * tk)], s_at("ag", mb, k, "r"))
-        ss = s_at("fw", mb, k, "s")
+        ss = s_at("fw", "s")
         piece = act.at[mb, k, at(c * four, four)]
         rdma(piece, piece, ss, s_at("fw", mb, k, "r"), core_peer)
-        sends.append((ss, act.at[mb, k, pl.ds(0, four)]))
 
     def spread_acts(mb, k):
         drain(act.at[mb, k, pl.ds(0, four)], s_at("fw", mb, k, "r"))
@@ -289,13 +340,13 @@
             def one(i, carry):
                 r = at(i * tile, tile)
                 sent[k, r, :] = new_grad(0, k, i * tile, tile)
-                rdma(sent.at[k, r], gs.at[1, k, r], s_at("shift", k, "s"), s_at("g", 1, k, "r"), before)
+                rdma(sent.at[k, r], gs.at[1, k, r], s_at("shift", "s"), s_at("g", 1, k, "r"), before)
                 return carry
 
             lax.fori_loop(0, rows // tile, one, 0)
 
     def give_back(k):
-        ss, rs = s_at("back", k, "s"), s_at("back", k, "r")
+        ss, rs = s_at("back", "s"), s_at("back", "r")
         for dx, dc in [(2, 0), (2, 1), (1, 0), (1, 1), (3, 0), (3, 1), (0, 1), (0, 0)]:
             px, pc, device = member(dx, dc)
             pos = (pc * NX + px) * tk
@@ -307,31 +358,29 @@
                     pltpu.make_async_copy(a, b, rs).start()
                 else:
                     rdma(a, b, ss, rs, device)
-        sends.append((ss, bk.at[k, pl.ds(0, rows - tk)]))
 
     def turn_x(mb, k):
         for i in range(wide // 256):
-            xt[i * 256 : (i + 1) * 256, :] = jnp.transpose(xs[mb, k, :, i * 256 : (i + 1) * 256])
+            xt[mb, k, i * 256 : (i + 1) * 256, :] = jnp.transpose(xs[mb, k, :, i * 256 : (i + 1) * 256])
 
     def turn_s(mb, k):
         for i in range(2 * hid // 256):
             sht[i * 256 : (i + 1) * 256, :] = jnp.transpose(shm[mb, k, :, i * 256 : (i + 1) * 256])
 
-    def grads(mb, k, first, last):
-        turn_x(mb, k)
+    def grads(mb, k):
+        first, last = (mb, k) == (0, 0), (mb, k) == (1, n_ch - 1)
         turn_s(mb, k)
         for h in (1, 0):
             hs = slice(h * half, (h + 1) * half)
             for j in range(4):
                 cs = slice(j * hid, (j + 1) * hid)
-                res = dot(xt[hs, :], amask[mb, k, :, cs])
+                res = dot(xt[mb, k, hs, :], amask[mb, k, :, cs])
                 if not first:
                     res = res + accgu[hs, cs]
                 if last and h == 1:
                     pgu[j] = (res * scale).astype(BF)
-                    ss = s_at("pgu", j, "s")
+                    ss = s_at("pgu", "s")
                     rdma(pgu.at[j], qgu.at[j], ss, s_at("pgu", j, "r"), y_peer)
-                    sends.append((ss, pgu.at[j]))
                 else:
                     accgu[hs, cs] = res
             for e in range(2):
@@ -341,9 +390,8 @@
                     res = res + accd[es, hs]
                 if last and h == 1:
                     pd[e] = (res * scale).astype(BF)
-                    ss = s_at("pd", e, "s")
+                    ss = s_at("pd", "s")
                     rdma(pd.at[e], qd.at[e], ss, s_at("pd", e, "r"), y_peer)
-                    sends.append((ss, pd.at[e]))
                 else:
                     accd[es, hs] = res
 
@@ -355,62 +403,54 @@
             drain(qd.at[e], s_at("pd", e, "r"))
             dd_ref[0, e] = accd[e * hid : (e + 1) * hid, 0:half] * scale + qd[e].astype(F32)
 
-    spread_meta()
-    weights()
-    for k in range(n_ch):
-        spread_x(0, k)
-        spread_g(k)
-    masks()
-    drain(wgu, s_at("wgu", "r"))
-    drain(wdn, s_at("wd", "r"))
-    for k in range(n_ch):
-        wait_x(0, k)
-        pre_gu(0, k)
-        wait_g(0, k)
-        pre_d(0, k)
-        mid_gu(0, k)
-        mid_d(0, k)
-        if k > 0:
-            activate(0, k - 1)
-    activate(0, n_ch - 1)
-    for k in range(n_ch):
-        spread_x(1, k)
-        spread_last(k)
-    for k in range(n_ch):
-        forward(0, k)
-        spread_acts(0, k)
-        relay(k)
-    for k in range(n_ch):
-        grads(0, k, k == 0, False)
-    for k in range(n_ch):
-        wait_x(1, k)
-        pre_gu(1, k)
-        mid_gu(1, k)
-    for k in range(n_ch):
-        wait_g(1, k)
-        pre_d(1, k)
-        mid_d(1, k)
-        activate(1, k)
-        forward(1, k)
-        spread_acts(1, k)
-        if k < n_ch - 1:
-            give_back(k)
-        grads(1, k, False, k == n_ch - 1)
-        if k == n_ch - 1:
-            give_back(k)
-    finish()
-    for k in range(n_ch):
-        @pl.when(sec > 0)
-        def _():
-            drain(sent.at[k], s_at("shift", k, "s"))
-
-        @pl.when(sec == n_sec - 1)
-        def _():
-            drain(gs.at[1, k, pl.ds(0, rows - tk)], s_at("last", k, "s"))
-        drain(bk.at[k], s_at("back", k, "r"))
+    steps = dict(
+        spread_meta=spread_meta, weights_gu=weights_gu, weights_d=weights_d, masks=masks,
+        wait_gu=wait_gu, wait_d=wait_d, turn_x=turn_x,
+        spread_x=spread_x, spread_g=spread_g, spread_last=spread_last, relay_last=relay_last,
+        wait_x=wait_x, wait_g=wait_g, pre_gu=pre_gu, pre_d=pre_d, mid_gu=mid_gu, mid_d=mid_d,
+        activate=activate, forward=forward, spread_acts=spread_acts, relay=relay,
+        give_back=give_back, grads=grads, finish=finish,
+    )
+    for name, *where in schedule(n_ch):
+        steps[name](*where)
+    @pl.when(sec > 0)
+    def _():
+        drain(sent, s_at("shift", "s"))
+
+    drain(bk, s_at("back", "r"))
+    for tag, ref in (
+        ("x", xs.at[:, :, pl.ds(0, rows - tk)]), ("g", gs.at[0, :, pl.ds(0, rows - tk)]),
+        ("p1gu", p1gu), ("p1d", p1d), ("s2gu", s2gu), ("s2d", s2d),
+        ("ag", act.at[:, :, pl.ds(0, 3 * tk)]), ("fw", act.at[:, :, pl.ds(0, four)]),
+        ("back", bk.at[:, pl.ds(0, rows - tk)]), ("pgu", pgu), ("pd", pd),
+    ):
+        drain(ref, s_at(tag, "s"))
+
+    @pl.when(lax.rem(sec, 2) == 1)
+    def _():
+        drain(glq.at[pl.ds(0, rows // 4 * n_ch - tok // 4)], s_at("last", "s"))
+
+    @pl.when((lax.rem(sec, 2) == 1) & (sec < n_sec - 1))
+    def _():
+        drain(glq, s_at("lastq", "s"))
+
     for s, ref in sends:
         drain(ref, s)
-    assert names.count <= n_sems, names.count
+    assert names.count == n_sems, names.count
+
+
+def write_out(*refs):
+    sem = refs[-1]
+    copies = []
+    for i in range(4):
+        rows = refs[i].shape[-2] // 4
+        for j in range(4):
+            part = (Ellipsis, pl.ds(j * rows, rows), slice(None))
+            copies.append(pltpu.make_async_copy(refs[i].at[part], refs[4 + i].at[part], sem.at[4 * i + j]))
+    for copy in copies:
+        copy.start()
+    for copy in copies:
+        copy.wait()
 
 
 def body(tokens_in, grad_first, grad_last, expert_ids, gate_probs, w_gate, w_up, w_down):
@@ -419,22 +459,20 @@
     wide = 2 * half
     tk = tok // CHUNKS
     rows, four = 2 * NX * tk, NX * tk
-    meta = jnp.concatenate(
-        [expert_ids[0, :, :, 0].astype(F32), gate_probs[0], jnp.zeros((4, tok), F32)], axis=0
-    )
-    n_sems = 40 + 44 * CHUNKS
+    n_sems = 20 + 20 * CHUNKS
     pair = (2, CHUNKS)
     scratch = [
         pltpu.VMEM(pair + (rows, wide), BF),
         pltpu.VMEM(pair + (rows, wide), BF),
+        pltpu.VMEM((2 * NX * tok // 4, wide), BF),
         pltpu.VMEM((CHUNKS, rows, wide), BF),
         pltpu.VMEM((CHUNKS, rows, wide), BF),
         pltpu.VMEM((wide, 4 * hid), BF),
         pltpu.VMEM((2 * hid, wide), BF),
-        pltpu.VMEM((2 * NX, 8, tok), F32),
+        pltpu.VMEM((2 * NX, 2, tok), jnp.int32),
         pltpu.VMEM(pair + (rows, 128), F32),
         pltpu.VMEM((2, tok, 128), F32),
-        pltpu.VMEM((wide, rows), BF),
+        pltpu.VMEM(pair + (wide, rows), BF),
         pltpu.VMEM((2 * hid, rows), BF),
         pltpu.VMEM(pair + (rows, 3 * hid), BF),
         pltpu.VMEM(pair + (rows, 4 * hid), BF),
@@ -459,7 +497,7 @@
     ]
     vmem = pl.BlockSpec(memory_space=pltpu.VMEM)
     hbm = pl.BlockSpec(memory_space=pl.ANY)
-    return pl.pallas_call(
+    results = pl.pallas_call(
         functools.partial(kernel, (wide, half, hid), tok, n_sems),
         out_shape=(
             jax.ShapeDtypeStruct((1, tok, width), BF),
@@ -467,14 +505,25 @@
             jax.ShapeDtypeStruct(w_up.shape, F32),
             jax.ShapeDtypeStruct(w_down.shape, F32),
         ),
-        in_specs=[hbm, hbm, hbm, vmem, hbm, hbm, hbm],
+        in_specs=[hbm, hbm, hbm, vmem, vmem, hbm, hbm, hbm],
         out_specs=(vmem,) * 4,
         scratch_shapes=scratch,
         compiler_params=pltpu.CompilerParams(
             collective_id=0, has_side_effects=True, vmem_limit_bytes=60 << 20
         ),
         name="section",
-    )(tokens_in, grad_first, grad_last, meta, w_gate, w_up, w_down)
+    )(
+        tokens_in, grad_first, grad_last, expert_ids.reshape(2, tok), gate_probs.reshape(2, tok),
+        w_gate, w_up, w_down,
+    )
+    return pl.pallas_call(
+        write_out,
+        out_shape=tuple(jax.ShapeDtypeStruct(r.shape, r.dtype) for r in results),
+        in_specs=[vmem] * 4,
+        out_specs=(hbm,) * 4,
+        scratch_shapes=[pltpu.SemaphoreType.DMA((16,))],
+        name="write_out",
+    )(*results)
 
 
 def solution(mesh):

time: 168 us -> 144 us (0.86)
  Pallas kernels: 159 us -> 142 us
  local copies, waits for them, and re-layouts: 6.02 us -> 0 us
  other arithmetic: 2.02 us -> 0 us
    pallas_call x1, Pallas kernels: 159 us -> 138 us  [body(): pl.pallas_call(functools.partial(kernel, (wide, half, hid), tok, n_sems),...]
    unnamed x10 -> x0, local copies, waits for them, and re-layouts: 5.94 us -> none
    pallas_call x0 -> x1, Pallas kernels: none -> 4.12 us  [body(): pl.pallas_call(write_out, out_shape=tuple((jax.ShapeDtypeStruct(r.shape,...]
where the time goes in v2:
time: 144 us; the launch traced here: 143 us
  Pallas kernels  142 us (99%)
    pallas_call x1, Pallas kernels, body(): pl.pallas_call(functools.partial(kernel, (wide, half, hid), tok, n_sems),...  138 us
    pallas_call x1, Pallas kernels, body(): pl.pallas_call(write_out, out_shape=tuple((jax.ShapeDtypeStruct(r.shape,...  4.12 us

profile of v2, /device:TPU:105, one launch (start us, length us, event | category | flops | bytes accessed | tf_op | source)
XLA Modules:
  0.0 142.8 jit_solution(13792156389693798148)
XLA Ops:
  0.6 137.8 %section.1 = (bf16[1,128,6144]{2,1,0:T(8,128)(2,1)}, f32[1,2,384,256]{3,2,1,0:T(8,128)}, f32[1,2,384,256]{3,2,1,0:T(8,128)}, f32[1,2,256,384]{3,2,1,0:T(8,128)}) custom-call(bf16[1,2,128,6144]{3,2,1,0:T(8,128)(2,1)} %x_ref.1, bf16[1,128,6144]{2,1,0:T(8,128)(2,1)} %g1_ref.1, bf16[128,6144]{1,0:T(8,128)(2,1)} %gl_ref.1, s32[2,128]{1,0:T(2,128)} %bitcast.2, ...), custom_call_target="tpu_custom_call" | custom-call | tf_op jit(solution)/shard_map/section/pallas_call | solution.py:500
  138.5 4.1 %write_out.1 = (bf16[1,128,6144]{2,1,0:T(8,128)(2,1)}, f32[1,2,384,256]{3,2,1,0:T(8,128)}, f32[1,2,384,256]{3,2,1,0:T(8,128)}, f32[1,2,256,384]{3,2,1,0:T(8,128)}) custom-call(bf16[1,128,6144]{2,1,0:T(8,128)(2,1)} %get-tuple-element.8.refs_0_, f32[1,2,384,256]{3,2,1,0:T(8,128)} %get-tuple-element.9.refs_1_, f32[1,2,384,256]{3,2,1,0:T(8,128)} %get-tuple-element.10.refs_2_, ...), custom_call_target="tpu_custom_call" | custom-call | tf_op jit(solution)/shard_map/write_out/pallas_call | solution.py:519

commit v3 on v2

--- a/solution.py
+++ b/solution.py
@@ -40,14 +40,14 @@
     ("spread_meta",), ("weights_gu",), ("spread_x", 0, 0), ("spread_g", 0), ("weights_d",), ("masks",),
     ("wait_x", 0, 0), ("spread_x", 0, 1), ("spread_last",),
     ("wait_gu",), ("pre_gu", 0, 0), ("mid_gu", 0, 0), ("turn_x", 0, 0), ("wait_g", 0, 0), ("wait_d",), ("pre_d", 0, 0), ("mid_d", 0, 0),
-    ("wait_x", 0, 1), ("pre_gu", 0, 1), ("activate", 0, 0), ("spread_g", 1), ("mid_gu", 0, 1), ("relay_last",),
-    ("forward", 0, 0), ("spread_acts", 0, 0), ("relay", 0),
+    ("wait_x", 0, 1), ("pre_gu", 0, 1), ("activate", 0, 0), ("spread_g", 1), ("relay_last",),
+    ("forward", 0, 0), ("mid_gu", 0, 1), ("spread_acts", 0, 0), ("relay", 0),
     ("turn_x", 0, 1), ("wait_g", 0, 1), ("pre_d", 0, 1), ("mid_d", 0, 1), ("activate", 0, 1), ("spread_x", 1, 0),
-    ("forward", 0, 1), ("spread_x", 1, 1), ("spread_acts", 0, 1), ("relay", 1), ("grads", 0, 0), ("grads", 0, 1),
+    ("forward", 0, 1), ("spread_acts", 0, 1), ("relay", 1), ("spread_x", 1, 1), ("grads", 0, 0), ("grads", 0, 1),
     ("wait_x", 1, 0), ("pre_gu", 1, 0), ("mid_gu", 1, 0), ("turn_x", 1, 0), ("wait_g", 1, 0), ("pre_d", 1, 0), ("mid_d", 1, 0),
     ("wait_x", 1, 1), ("pre_gu", 1, 1), ("mid_gu", 1, 1), ("activate", 1, 0), ("turn_x", 1, 1),
-    ("wait_g", 1, 1), ("pre_d", 1, 1), ("forward", 1, 0), ("mid_d", 1, 1), ("spread_acts", 1, 0),
-    ("activate", 1, 1), ("grads", 1, 0), ("forward", 1, 1), ("spread_acts", 1, 1), ("grads", 1, 1), ("give_back", 0), ("give_back", 1), ("finish",),
+    ("wait_g", 1, 1), ("pre_d", 1, 1), ("mid_d", 1, 1), ("forward", 1, 0),
+    ("activate", 1, 1), ("spread_acts", 1, 0), ("grads", 1, 0), ("forward", 1, 1), ("spread_acts", 1, 1), ("grads", 1, 1), ("give_back", 0), ("give_back", 1), ("finish",),
 ]
 
 
@@ -61,7 +61,7 @@
     back_ref, dg_ref, du_ref, dd_ref,
     xs, gs, glq, sent, bk, wgu, wdn, metas, msk, prob, xt, sht, act, amask, shm,
     p1gu, r1gu, owngu, s2gu, r2gu, p1d, r1d, ownd, s2d, r2d,
-    accgu, accd, pgu, pd, qgu, qd, sem,
+    accgu, accd, pgu, pd, qgu, qd, outgu, outd, sem,
 ):
     wide, half, hid = dims
     n_ch = CHUNKS
@@ -120,10 +120,10 @@
 
     @pl.when(sec == n_sec - 1)
     def _():
-        for q in range(3):
-            pl.semaphore_signal(bar, inc=1, device_id=(dp, 2 * q + 1), device_id_type=MESH)
-
-    helper = jnp.where((lax.rem(sec, 2) == 1) & (sec < n_sec - 1), 1, 0)
+        for q in range(7):
+            pl.semaphore_signal(bar, inc=1, device_id=(dp, q), device_id_type=MESH)
+
+    helper = jnp.where(sec < n_sec - 1, 1, 0)
     pl.semaphore_wait(bar, len(offsets) + 2 + helper)
 
     def spread_meta():
@@ -187,17 +187,17 @@
         ss = s_at("g", "s")
         spread(g1_ref.at[0], gs.at[0, k], k * tk, tk, block * tk, ss, s_at("g", 0, k, "r"))
 
-    def quarter(q):
-        per = 4 // n_ch
+    def eighth(q):
+        per = 8 // n_ch
         size = tk // per
         return q // per, (q % per) * size, size
 
     def spread_last():
-        for q in range(4):
-            @pl.when(sec == 2 * q + 1)
+        for q in range(8):
+            @pl.when(sec == q)
             def _():
-                k, base, size = quarter(q)
-                if q < 3:
+                k, base, size = eighth(q)
+                if q < 7:
                     rs = s_at("lastq", "r")
                     spread(gl_ref, glq, k * tk + base, size, block * size, s_at("last", "s"), rs)
                 else:
@@ -205,10 +205,10 @@
                     spread(gl_ref, gs.at[1, k], k * tk + base, size, block * tk + base, s_at("last", "s"), rs)
 
     def relay_last():
-        for q in range(3):
-            @pl.when(sec == 2 * q + 1)
+        for q in range(7):
+            @pl.when(sec == q)
             def _():
-                k, base, size = quarter(q)
+                k, base, size = eighth(q)
                 drain(glq, s_at("lastq", "r"))
                 for b in range(2 * NX):
                     rdma(
@@ -398,10 +398,14 @@
     def finish():
         for j, (ref, e) in enumerate([(dg_ref, 0), (dg_ref, 1), (du_ref, 0), (du_ref, 1)]):
             drain(qgu.at[j], s_at("pgu", j, "r"))
-            ref[0, e] = accgu[0:half, j * hid : (j + 1) * hid] * scale + qgu[j].astype(F32)
+            outgu[j] = accgu[0:half, j * hid : (j + 1) * hid] * scale + qgu[j].astype(F32)
+            pltpu.make_async_copy(outgu.at[j], ref.at[0, e], s_at("out")).start()
         for e in range(2):
             drain(qd.at[e], s_at("pd", e, "r"))
-            dd_ref[0, e] = accd[e * hid : (e + 1) * hid, 0:half] * scale + qd[e].astype(F32)
+            outd[e] = accd[e * hid : (e + 1) * hid, 0:half] * scale + qd[e].astype(F32)
+            pltpu.make_async_copy(outd.at[e], dd_ref.at[0, e], s_at("outd")).start()
+        drain(outgu, s_at("out"))
+        drain(outd, s_at("outd"))
 
     steps = dict(
         spread_meta=spread_meta, weights_gu=weights_gu, weights_d=weights_d, masks=masks,
@@ -426,11 +430,9 @@
     ):
         drain(ref, s_at(tag, "s"))
 
-    @pl.when(lax.rem(sec, 2) == 1)
-    def _():
-        drain(glq.at[pl.ds(0, rows // 4 * n_ch - tok // 4)], s_at("last", "s"))
-
-    @pl.when((lax.rem(sec, 2) == 1) & (sec < n_sec - 1))
+    drain(glq.at[pl.ds(0, tok - tok // 8)], s_at("last", "s"))
+
+    @pl.when(sec < n_sec - 1)
     def _():
         drain(glq, s_at("lastq", "s"))
 
@@ -440,17 +442,24 @@
 
 
 def write_out(*refs):
-    sem = refs[-1]
-    copies = []
+    held, got, put = refs[8:12], refs[12], refs[13]
+    parts = []
     for i in range(4):
-        rows = refs[i].shape[-2] // 4
-        for j in range(4):
+        rows = refs[i].shape[-2] // 2
+        for j in range(2):
             part = (Ellipsis, pl.ds(j * rows, rows), slice(None))
-            copies.append(pltpu.make_async_copy(refs[i].at[part], refs[4 + i].at[part], sem.at[4 * i + j]))
-    for copy in copies:
-        copy.start()
-    for copy in copies:
-        copy.wait()
+            n = 2 * i + j
+            parts.append((
+                pltpu.make_async_copy(refs[i].at[part], held[i].at[part], got.at[n]),
+                pltpu.make_async_copy(held[i].at[part], refs[4 + i].at[part], put.at[n]),
+            ))
+    for first, _ in parts:
+        first.start()
+    for first, second in parts:
+        first.wait()
+        second.start()
+    for _, second in parts:
+        second.wait()
 
 
 def body(tokens_in, grad_first, grad_last, expert_ids, gate_probs, w_gate, w_up, w_down):
@@ -459,12 +468,12 @@
     wide = 2 * half
     tk = tok // CHUNKS
     rows, four = 2 * NX * tk, NX * tk
-    n_sems = 20 + 20 * CHUNKS
+    n_sems = 22 + 20 * CHUNKS
     pair = (2, CHUNKS)
     scratch = [
         pltpu.VMEM(pair + (rows, wide), BF),
         pltpu.VMEM(pair + (rows, wide), BF),
-        pltpu.VMEM((2 * NX * tok // 4, wide), BF),
+        pltpu.VMEM((2 * NX * tok // 8, wide), BF),
         pltpu.VMEM((CHUNKS, rows, wide), BF),
         pltpu.VMEM((CHUNKS, rows, wide), BF),
         pltpu.VMEM((wide, 4 * hid), BF),
@@ -493,6 +502,8 @@
         pltpu.VMEM((2, hid, half), BF),
         pltpu.VMEM((4, half, hid), BF),
         pltpu.VMEM((2, hid, half), BF),
+        pltpu.VMEM((4, half, hid), F32),
+        pltpu.VMEM((2, hid, half), F32),
         pltpu.SemaphoreType.DMA((n_sems,)),
     ]
     vmem = pl.BlockSpec(memory_space=pltpu.VMEM)
@@ -506,7 +517,7 @@
             jax.ShapeDtypeStruct(w_down.shape, F32),
         ),
         in_specs=[hbm, hbm, hbm, vmem, vmem, hbm, hbm, hbm],
-        out_specs=(vmem,) * 4,
+        out_specs=(hbm,) * 4,
         scratch_shapes=scratch,
         compiler_params=pltpu.CompilerParams(
             collective_id=0, has_side_effects=True, vmem_limit_bytes=60 << 20
@@ -519,9 +530,10 @@
     return pl.pallas_call(
         write_out,
         out_shape=tuple(jax.ShapeDtypeStruct(r.shape, r.dtype) for r in results),
-        in_specs=[vmem] * 4,
+        in_specs=[hbm] * 4,
         out_specs=(hbm,) * 4,
-        scratch_shapes=[pltpu.SemaphoreType.DMA((16,))],
+        scratch_shapes=[pltpu.VMEM(r.shape, r.dtype) for r in results]
+        + [pltpu.SemaphoreType.DMA((8,))] * 2,
         name="write_out",
     )(*results)
 

time: 144 us -> 140 us (0.972)
  the two profiles are of different devices: /device:TPU:105 before, /device:TPU:1 now
where the time goes in v3:
time: 140 us
  Pallas kernels  139 us (99%)
    pallas_call x1, Pallas kernels, body(): pl.pallas_call(functools.partial(kernel, (wide, half, hid), tok, n_sems),...  136 us
    pallas_call x1, Pallas kernels, body(): pl.pallas_call(write_out, out_shape=tuple((jax.ShapeDtypeStruct(r.shape,...  3.18 us

profile of v3, /device:TPU:1, one launch (start us, length us, event | category | flops | bytes accessed | tf_op | source)
XLA Modules:
  0.0 140.0 jit_solution(17465349522368864799)
XLA Ops:
  0.6 136.1 %section.1 = (bf16[1,128,6144]{2,1,0:T(8,128)(2,1)}, f32[1,2,384,256]{3,2,1,0:T(8,128)}, f32[1,2,384,256]{3,2,1,0:T(8,128)}, f32[1,2,256,384]{3,2,1,0:T(8,128)}) custom-call(bf16[1,2,128,6144]{3,2,1,0:T(8,128)(2,1)} %x_ref.1, bf16[1,128,6144]{2,1,0:T(8,128)(2,1)} %g1_ref.1, bf16[128,6144]{1,0:T(8,128)(2,1)} %gl_ref.1, s32[2,128]{1,0:T(2,128)} %bitcast.2, ...), custom_call_target="tpu_custom_call" | custom-call | tf_op jit(solution)/shard_map/section/pallas_call | solution.py:511
  136.7 3.2 %write_out.1 = (bf16[1,128,6144]{2,1,0:T(8,128)(2,1)}, f32[1,2,384,256]{3,2,1,0:T(8,128)}, f32[1,2,384,256]{3,2,1,0:T(8,128)}, f32[1,2,256,384]{3,2,1,0:T(8,128)}) custom-call(bf16[1,128,6144]{2,1,0:T(8,128)(2,1)} %get-tuple-element.8.refs_0_, f32[1,2,384,256]{3,2,1,0:T(8,128)} %get-tuple-element.9.refs_1_, f32[1,2,384,256]{3,2,1,0:T(8,128)} %get-tuple-element.10.refs_2_, ...), custom_call_target="tpu_custom_call" | custom-call | tf_op jit(solution)/shard_map/write_out/pallas_call | solution.py:530
